TPU v7x, 32 devices: a whole 2x2x4 slice. The times are simulated.
32 devices in a mesh: particle: 4 (over z), tile: 8 (over y, x, core).
Axes of the slice: x: 2, y: 2, z: 4, core: 2. Of those that a mesh axis runs over, the one named last changes fastest.
Arguments:
- biomass: float32 [16, 32768], P('particle', 'tile'), as said below
- water: float32 [16, 32768], P('particle', 'tile'), may hold values from -5 to 5
- flow_blocks: bfloat16 [256, 3, 128, 128], P('tile'), may hold values from -0.15625 to 0.15625
- neighbours: int32 [256, 3], P('tile'), may hold values from 0 to 255, as said below
- rain: float32 [4, 16, 32768], P(None, 'particle', 'tile'), may hold values from -4 to 4
- growth_rate: float32 [32768], P('tile'), may hold values from 0.05 to 0.5
- observations: float32 [2, 32768], P(None, 'tile'), may hold values from -5 to 5
- obs_precision: float32 [32768], P('tile'), as said below
- ancestors: int32 [2, 16], replicated, may hold values from 0 to 15
Outputs:
- means: float32 [2, 2, 32768], P(None, None, 'tile')
- biomass_out: float32 [16, 32768], P('particle', 'tile')
- water_out: float32 [16, 32768], P('particle', 'tile')
Inputs may be any that keep to these rules, and one draw needn't show every extreme that they name: `neighbours`: row n lists block n first, then one block 1 to 4 blocks below n and one 1 to 4 blocks above n, each clipped to the grid's ends. `biomass`: every entry lies between 0.5 and 2. `obs_precision`: every entry lies between 0.3 / sqrt(32768) and 3 / sqrt(32768).
All inputs are finite; a program needn't handle non-finite values.
Results may differ from a plain program's by a relative error of at most 0.0019.
Values may be sent and summed in bfloat16 or wider, within the bound.
No kernel may reach another device: no remote copies, remote signals or barrier semaphores. Data moves between devices by JAX's collectives and lax.ppermute only.
A program may use at most 64 MiB of HBM per device.

v0:
```python
import jax
import jax.numpy as jnp
from jax import lax
from jax.sharding import PartitionSpec as P

BLK = 128
CYCLES = 2
DAYS = 2
HALO = 4


def padded(cells, sides, width):
    for axis, dim in sides:
        count = lax.axis_size(axis)
        ends = count - 1
        head = lax.slice_in_dim(cells, 0, width, axis=dim)
        tail = lax.slice_in_dim(cells, cells.shape[dim] - width, cells.shape[dim], axis=dim)
        cells = jnp.concatenate(
            [
                lax.ppermute(tail, axis, [(i, (i + 1) % count) for i in range(ends)]),
                cells,
                lax.ppermute(head, axis, [((i + 1) % count, i) for i in range(ends)]),
            ],
            axis=dim,
        )
    return cells


def body(
    biomass,
    water,
    flow_blocks,
    neighbours,
    rain,
    growth_rate,
    observations,
    obs_precision,
    ancestors,
):
    part_dev = biomass.shape[0]
    cells = biomass.shape[1]
    blocks_dev = cells // BLK
    member = lax.axis_index("particle")
    tile_pos = lax.axis_index("tile")
    local_ids = neighbours - tile_pos * blocks_dev + HALO
    bio, wat = (biomass, water)
    collected = []
    for cycle in range(CYCLES):
        misfit_local = -0.5 * jnp.sum(obs_precision * (bio - observations[cycle]) ** 2, axis=1)
        summed = lax.psum(misfit_local, "tile")
        log_weight = lax.all_gather(summed, "particle", axis=0, tiled=True)
        shifted = jnp.exp(log_weight - jnp.max(log_weight))
        weight = shifted / jnp.sum(shifted)
        my_weight = lax.dynamic_slice_in_dim(weight, member * part_dev, part_dev)
        partial_sums = jnp.stack(
            [jnp.sum(my_weight[:, None] * bio, axis=0), jnp.sum(my_weight[:, None] * wat, axis=0)]
        )
        collected.append(lax.psum(partial_sums, "particle"))
        chosen = ancestors[cycle]
        mine = lax.dynamic_slice_in_dim(chosen, member * part_dev, part_dev)
        piece = (
            lax.all_gather(bio, "particle", axis=0, tiled=True),
            lax.all_gather(wat, "particle", axis=0, tiled=True),
        )
        count = piece[0].shape[0]
        hit = jnp.arange(count, dtype=jnp.int32)[None, :] == mine[:, None]
        bio, wat = tuple(
            (jnp.sum(jnp.where(hit[:, :, None], rows[None], 0.0), axis=1) for rows in piece)
        )
        for day in range(DAYS):
            wb = wat.astype(jnp.bfloat16).reshape(part_dev, blocks_dev, BLK)
            extended = padded(wb, (("tile", 1),), HALO)
            nearby = extended[:, local_ids]
            flux = jnp.einsum(
                "pnkc,nkdc->pnd", nearby, flow_blocks, preferred_element_type=jnp.float32
            ).reshape(part_dev, cells)
            wet = wat * wat / (1.0 + wat * wat)
            new_bio = bio + growth_rate * bio * (wet - 0.4 * bio)
            new_wat = wat + flux + rain[cycle * DAYS + day] - 0.2 * bio * wet
            bio = new_bio
            wat = new_wat
    return (jnp.stack(collected), bio, wat)


def solution(mesh):
    placed = (
        P("particle", "tile"),
        P("particle", "tile"),
        P("tile", None, None, None),
        P("tile", None),
        P(None, "particle", "tile"),
        P("tile"),
        P(None, "tile"),
        P("tile"),
        P(),
    )
    return jax.shard_map(
        body,
        mesh=mesh,
        in_specs=placed,
        out_specs=(P(None, None, "tile"), P("particle", "tile"), P("particle", "tile")),
        check_vma=False,
    )
```

profile of v0, /device:TPU:0, one launch (start us, length us, event | category | flops | bytes accessed | tf_op | source)
XLA Modules:
  0.0 191.6 jit_solution(2245552599224987325)
XLA Ops:
  8.2 15.8 %all-gather = f32[4,4,4096]{2,1,0:T(4,128)S(1)} all-gather(f32[1,4,4096]{2,1,0:T(4,128)} %bitcast.146), channel_id=1, replica_groups=mesh['particle'=4,'tile'=8] {'particle'}, dimensions={0}, use_global_device_ids=true | all-gather | bytes 327680 | tf_op jit(solution)/shard_map/all_gather | solution.py:62
  24.8 14.9 %all-gather.1 = f32[4,4,4096]{2,1,0:T(4,128)S(1)} all-gather(f32[1,4,4096]{2,1,0:T(4,128)} %bitcast.152), channel_id=1, replica_groups=mesh['particle'=4,'tile'=8] {'particle'}, dimensions={0}, use_global_device_ids=true | all-gather | bytes 327680 | tf_op jit(solution)/shard_map/all_gather | solution.py:63
  40.5 1.5 select_reduce_fusion.3
  43.3 1.3 collective-permute-start.1
  49.1 1.3 gather_fusion
  50.4 2.9 %multiply_reduce_fusion.5 = (f32[4]{0:T(128)S(1)}, f32[4]{0:T(128)S(1)}, f32[4,4096]{1,0:T(4,128)}, f32[4,4096]{1,0:T(4,128)}, f32[32,4,128,1]{2,1,3,0:T(4,128)S(1)}) fusion(f32[4,4096]{1,0:T(4,128)} %param.9, f32[4096]{0:T(1024)S(1)} %bitcast.156, f32[4096]{0:T(1024)} %param.16, f32[4096]{0:T(1024)S(1)} %bitcast.155, f32[4,4096]{1,0:T(4,128)S(1)} %get-tuple-element.11, ...), kind=kOutput, calls=%fused_computation.50 | convolution fusion | flops 13058040 | bytes 3768352 | tf_op jit(solution)/shard_map/pnkc,nkdc->pnd/dot_general | solution.py:74
  54.9 4.7 %collective-permute-start.2 = (bf16[4,4,128]{2,0,1:T(4,128)(2,1)}, bf16[4,4,128]{2,0,1:T(4,128)(2,1)S(1)}, u32[]{:S(2)}, u32[]{:S(2)}) collective-permute-start(bf16[4,4,128]{2,0,1:T(4,128)(2,1)} %get-tuple-element.27), channel_id=1, source_target_pairs={{0,1},{1,2},{2,3},{3,4},{4,5},{5,6},{6,7},{8,9},{9,10},{10,11},{11... | collective-permute-start | bytes 12296 | tf_op jit(solution)/shard_map/ppermute | solution.py:20
  61.0 15.7 %all-reduce.2 = (f32[4]{0:T(128)S(1)}, f32[4]{0:T(128)S(1)}) all-reduce(f32[4]{0:T(128)S(1)} %get-tuple-element.38, f32[4]{0:T(128)S(1)} %get-tuple-element.39), channel_id=1, replica_groups=mesh['particle'=4,'tile'=8] {'tile'}, use_global_device_ids=true, to_apply=%region_10.11 | all-reduce | flops 8 | bytes 64 | tf_op jit(solution)/shard_map/psum | solution.py:50
  77.1 11.5 %all-reduce.4 = (f32[16]{0:T(128)S(1)}, f32[16]{0:T(128)S(1)}) all-reduce(f32[16]{0:T(128)S(1)} %dynamic-update-slice.1, f32[16]{0:T(128)S(1)} %dynamic-update-slice), channel_id=1, replica_groups=mesh['particle'=4,'tile'=8] {'particle'}, use_global_device_ids=true, to_apply=%add.1 | all-reduce | flops 32 | bytes 256
  89.3 1.4 fusion.17
  90.7 1.4 broadcast_divide_fusion
  92.7 1.4 fusion.16
  94.1 1.4 broadcast_divide_fusion.1
  96.3 14.1 %all-gather.2 = f32[4,4,4096]{2,1,0:T(4,128)S(1)} all-gather(f32[1,4,4096]{2,1,0:T(4,128)} %bitcast.145), channel_id=1, replica_groups=mesh['particle'=4,'tile'=8] {'particle'}, dimensions={0}, use_global_device_ids=true | all-gather | bytes 327680 | tf_op jit(solution)/shard_map/all_gather | solution.py:62
  113.4 2.1 %multiply_reduce_fusion.1 = (f32[4096]{0:T(1024)S(1)}, f32[4096]{0:T(1024)S(1)}, f32[4,4096]{1,0:T(4,128)S(1)}) fusion(f32[4,4096]{1,0:T(4,128)} %get-tuple-element.21, f32[4]{0:T(128)} %dynamic_slice.14, f32[4,4096]{1,0:T(4,128)} %get-tuple-element.22, f32[4,4096]{1,0:T(4,128)S(1)} %get-tuple-element.11, f32[4,4096]{1,0:T(4,128)S(1)} %get-tuple-element.12, ...), kind=kOutput, calls=%fused_computation.44 | convolution fusion | flops 12902400 | bytes 3686416 | tf_op jit(solution)/shard_map/pnkc,nkdc->pnd/dot_general | solution.py:74
  115.5 13.8 %all-gather.3 = f32[4,4,4096]{2,1,0:T(4,128)S(1)} all-gather(f32[1,4,4096]{2,1,0:T(4,128)S(1)} %bitcast.151), channel_id=1, replica_groups=mesh['particle'=4,'tile'=8] {'particle'}, dimensions={0}, use_global_device_ids=true | all-gather | bytes 327680 | tf_op jit(solution)/shard_map/all_gather | solution.py:63
  130.1 1.5 select_reduce_fusion.1
  134.2 1.4 maximum_bitcast_fusion
  137.2 2.7 %multiply_add_fusion = (f32[4,4096]{1,0:T(4,128)}, f32[4,4096]{1,0:T(4,128)S(1)}, f32[32,4,128,1]{2,1,3,0:T(4,128)S(1)}) fusion(f32[4096]{0:T(1024)S(1)} %copy-done.2, f32[4,4096]{1,0:T(4,128)S(1)} %get-tuple-element.5, f32[4,4096]{1,0:T(4,128)S(1)} %get-tuple-element.6, f32[4,4,4096]{2,1,0:T(4,128)} %param.13, bf16[4,32,3,128]{3,0,2,1:T(4,128)(2,1)S(1)} %bitcast.150, ...), kind=kOutput, calls=%fused_computation.41 | convolution fusion | flops 12926976 | bytes 3653632 | tf_op jit(solution)/shard_map/pnkc,nkdc->pnd/dot_general | solution.py:74
  140.8 4.3 %collective-permute-start.6 = (bf16[4,4,128]{2,0,1:T(4,128)(2,1)S(1)}, bf16[4,4,128]{2,0,1:T(4,128)(2,1)S(1)}, u32[]{:S(2)}, u32[]{:S(2)}) collective-permute-start(bf16[4,4,128]{2,0,1:T(4,128)(2,1)S(1)} %get-tuple-element.23), channel_id=1, source_target_pairs={{0,1},{1,2},{2,3},{3,4},{4,5},{5,6},{6,7},{8,9},{9,10},{10,11},{11... | collective-permute-start | bytes 12296 | tf_op jit(solution)/shard_map/ppermute | solution.py:20
  147.1 1.8 collective-permute-done.7
  149.7 2.7 %fusion.2 = f32[4,4096]{1,0:T(4,128)} fusion(f32[4,4096]{1,0:T(4,128)S(1)} %get-tuple-element.20, bf16[4,32,3,128]{3,0,2,1:T(4,128)(2,1)S(1)} %bitcast.147, bf16[32,3,128,128]{3,2,1,0:T(8,128)(2,1)S(1)} %copy-done, f32[4,4,4096]{2,1,0:T(4,128)} %param.13, f32[4,4096]{1,0:T(4,128)S(1)} %get-tuple-element.5, f32[4,4096]{1,0:T(4,128)S(1)} %get-tuple-element.6, ...), kind=kOutput, calls=%fused_computation.7 | convolution fusion | flops 12845056 | bytes 3588096 | tf_op jit(solution)/shard_map/pnkc,nkdc->pnd/dot_general | solution.py:74
  152.3 31.0 %all-reduce.7.cloned.1.call-done = (f32[1,2,4096]{2,1,0:T(2,128)}, f32[1,2,4096]{2,1,0:T(2,128)}) async-done(((f32[1,2,4096]{2,1,0:T(2,128)}, f32[1,2,4096]{2,1,0:T(2,128)}), (f32[1,2,4096]{2,1,0:T(2,128)}, f32[1,2,4096]{2,1,0:T(2,128)})) %all-reduce.7.cloned.1.call-update) | async-done | bytes 65552 | tf_op jit(solution)/shard_map/psum | solution.py:58
  183.4 1.4 pad_maximum_fusion
  (67 shorter events, 24.7 us)
Async XLA Ops:
  7.2 43.3 %copy-start = (bf16[32,3,128,128]{3,2,1,0:T(8,128)(2,1)S(1)}, bf16[32,3,128,128]{3,2,1,0:T(8,128)(2,1)}, u32[]{:S(2)}) copy-start(bf16[32,3,128,128]{3,2,1,0:T(8,128)(2,1)} %param.11) | copy-start | bytes 9437188
  7.2 176.2 %all-reduce.7.cloned.1.call-start = ((), (), s32[]{:S(2)}) async-start(), calls=%async_computation | async-start | bytes 131072 | tf_op jit(solution)/shard_map/psum | solution.py:58
  24.8 70.7 %copy-start.1 = (f32[4,4096]{1,0:T(4,128)S(1)}, f32[4,4096]{1,0:T(4,128)}, u32[]{:S(2)}) copy-start(f32[4,4096]{1,0:T(4,128)} %param.9) | copy-start | bytes 196612
  24.8 70.7 %copy-start.3 = (f32[4,4096]{1,0:T(4,128)S(1)}, f32[4,4096]{1,0:T(4,128)}, u32[]{:S(2)}) copy-start(f32[4,4096]{1,0:T(4,128)} %param.10) | copy-start | bytes 196612
  42.0 7.0 %collective-permute-start = (bf16[4,4,128]{2,0,1:T(4,128)(2,1)S(1)}, bf16[4,4,128]{2,0,1:T(4,128)(2,1)S(1)}, u32[]{:S(2)}, u32[]{:S(2)}) collective-permute-start(bf16[4,4,128]{2,0,1:T(4,128)(2,1)S(1)} %get-tuple-element.29), channel_id=1, source_target_pairs={{0,1},{1,2},{2,3},{3,4},{4,5},{5,6},{6,7},{8,9},{9,10},{10,11},{11... | collective-permute-start | bytes 12296 | tf_op jit(solution)/shard_map/ppermute | solution.py:20
  43.3 5.7 %collective-permute-start.1 = (bf16[4,4,128]{2,0,1:T(4,128)(2,1)S(1)}, bf16[4,4,128]{2,0,1:T(4,128)(2,1)S(1)}, u32[]{:S(2)}, u32[]{:S(2)}) collective-permute-start(bf16[4,4,128]{2,0,1:T(4,128)(2,1)S(1)} %get-tuple-element.30), channel_id=1, source_target_pairs={{1,0},{2,1},{3,2},{4,3},{5,4},{6,5},{7,6},{9,8},{10,9},{11,10},{12... | collective-permute-start | bytes 12296 | tf_op jit(solution)/shard_map/ppermute | solution.py:22
  54.3 42.0 %copy-start.4 = (bf16[4,32,128]{2,0,1:T(4,128)(2,1)}, bf16[4,32,128]{2,0,1:T(4,128)(2,1)S(1)}, u32[]{:S(2)}) copy-start(bf16[4,32,128]{2,0,1:T(4,128)(2,1)S(1)} %fusion.14) | copy-start | bytes 98308
  54.9 57.0 %collective-permute-start.2 = (bf16[4,4,128]{2,0,1:T(4,128)(2,1)}, bf16[4,4,128]{2,0,1:T(4,128)(2,1)S(1)}, u32[]{:S(2)}, u32[]{:S(2)}) collective-permute-start(bf16[4,4,128]{2,0,1:T(4,128)(2,1)} %get-tuple-element.27), channel_id=1, source_target_pairs={{0,1},{1,2},{2,3},{3,4},{4,5},{5,6},{6,7},{8,9},{9,10},{10,11},{11... | collective-permute-start | bytes 12296 | tf_op jit(solution)/shard_map/ppermute | solution.py:20
  59.6 52.2 %collective-permute-start.3 = (bf16[4,4,128]{2,0,1:T(4,128)(2,1)}, bf16[4,4,128]{2,0,1:T(4,128)(2,1)}, u32[]{:S(2)}, u32[]{:S(2)}) collective-permute-start(bf16[4,4,128]{2,0,1:T(4,128)(2,1)} %get-tuple-element.28), channel_id=1, source_target_pairs={{1,0},{2,1},{3,2},{4,3},{5,4},{6,5},{7,6},{9,8},{10,9},{11,10},{12... | collective-permute-start | bytes 12296 | tf_op jit(solution)/shard_map/ppermute | solution.py:22
  111.8 22.4 %copy-start.5 = (f32[4096]{0:T(1024)S(1)}, f32[4096]{0:T(1024)}, u32[]{:S(2)}) copy-start(f32[4096]{0:T(1024)} %get-tuple-element.7) | copy-start | bytes 49156
  111.8 25.4 %copy-start.2 = (f32[4096]{0:T(1024)S(1)}, f32[4096]{0:T(1024)}, u32[]{:S(2)}) copy-start(f32[4096]{0:T(1024)} %param.14) | copy-start | bytes 49156
  131.6 4.0 %collective-permute-start.4 = (bf16[4,4,128]{2,0,1:T(4,128)(2,1)S(1)}, bf16[4,4,128]{2,0,1:T(4,128)(2,1)S(1)}, u32[]{:S(2)}, u32[]{:S(2)}) collective-permute-start(bf16[4,4,128]{2,0,1:T(4,128)(2,1)S(1)} %get-tuple-element.25), channel_id=1, source_target_pairs={{0,1},{1,2},{2,3},{3,4},{4,5},{5,6},{6,7},{8,9},{9,10},{10,11},{11... | collective-permute-start | bytes 12296 | tf_op jit(solution)/shard_map/ppermute | solution.py:20
  132.9 3.5 %collective-permute-start.5 = (bf16[4,4,128]{2,0,1:T(4,128)(2,1)S(1)}, bf16[4,4,128]{2,0,1:T(4,128)(2,1)S(1)}, u32[]{:S(2)}, u32[]{:S(2)}) collective-permute-start(bf16[4,4,128]{2,0,1:T(4,128)(2,1)S(1)} %get-tuple-element.26), channel_id=1, source_target_pairs={{1,0},{2,1},{3,2},{4,3},{5,4},{6,5},{7,6},{9,8},{10,9},{11,10},{12... | collective-permute-start | bytes 12296 | tf_op jit(solution)/shard_map/ppermute | solution.py:22
  140.8 6.3 %collective-permute-start.6 = (bf16[4,4,128]{2,0,1:T(4,128)(2,1)S(1)}, bf16[4,4,128]{2,0,1:T(4,128)(2,1)S(1)}, u32[]{:S(2)}, u32[]{:S(2)}) collective-permute-start(bf16[4,4,128]{2,0,1:T(4,128)(2,1)S(1)} %get-tuple-element.23), channel_id=1, source_target_pairs={{0,1},{1,2},{2,3},{3,4},{4,5},{5,6},{6,7},{8,9},{9,10},{10,11},{11... | collective-permute-start | bytes 12296 | tf_op jit(solution)/shard_map/ppermute | solution.py:20
  145.1 3.8 %collective-permute-start.7 = (bf16[4,4,128]{2,0,1:T(4,128)(2,1)S(1)}, bf16[4,4,128]{2,0,1:T(4,128)(2,1)S(1)}, u32[]{:S(2)}, u32[]{:S(2)}) collective-permute-start(bf16[4,4,128]{2,0,1:T(4,128)(2,1)S(1)} %get-tuple-element.24), channel_id=1, source_target_pairs={{1,0},{2,1},{3,2},{4,3},{5,4},{6,5},{7,6},{9,8},{10,9},{11,10},{12... | collective-permute-start | bytes 12296 | tf_op jit(solution)/shard_map/ppermute | solution.py:22
Sparse Core Ops, SparseCore 0:
  147.2 36.1 all-reduce.6
where the time goes:
time: 193 us; the launch traced here: 192 us
  blocking collectives  85.8 us (44%)
  waiting for transfers between devices  33.8 us (18%)
  other arithmetic  18.2 us (9%)
  starting transfers between devices  16.8 us (9%)
  between operations  15 us (8%)
  local copies, waits for them, and re-layouts  11.7 us (6%)
  matrix products  10.5 us (5%)
    psum x1, waiting for transfers between devices, body(): collected.append(lax.psum(partial_sums, 'particle'))  31 us
    all_gather x2, blocking collectives, body(): lax.all_gather(bio, 'particle', axis=0, tiled=True)  29.9 us
    all_gather x2, blocking collectives, body(): lax.all_gather(wat, 'particle', axis=0, tiled=True)  28.7 us
    psum x1, blocking collectives, body(): summed = lax.psum(misfit_local, 'tile')  15.7 us
    ppermute x4, starting transfers between devices, padded(): lax.ppermute(tail, axis, [(i, (i + 1) % count) for i in range(ends)])  11.6 us
    unnamed x1, blocking collectives  11.5 us
    dot_general x4, matrix products, body(): jnp.einsum('pnkc,nkdc->pnd', nearby, flow_blocks, preferred_element_type=...  10.5 us
    ppermute x4, starting transfers between devices, padded(): lax.ppermute(head, axis, [((i + 1) % count, i) for i in range(ends)])  5.17 us
  transfers between devices with their start and end apart: 9, of which 3 were waited for; matrix products, arithmetic and copies ran while one was open for 10% of the time, Pallas kernels for 0%

commit v1 on v0

--- a/solution.py
+++ b/solution.py
@@ -7,6 +7,18 @@
 CYCLES = 2
 DAYS = 2
 HALO = 4
+
+
+def doubled_up(shard, axis, dim):
+    ways, here = (lax.axis_size(axis), lax.axis_index(axis))
+    grown, reach = (shard, 1)
+    while reach < ways:
+        theirs = lax.ppermute(grown, axis, [(d, d ^ reach) for d in range(ways)])
+        mine_first = jnp.concatenate([grown, theirs], axis=dim)
+        theirs_first = jnp.concatenate([theirs, grown], axis=dim)
+        grown = jnp.where(here & reach == 0, mine_first, theirs_first)
+        reach = 2 * reach
+    return grown
 
 
 def padded(cells, sides, width):
@@ -59,7 +71,7 @@
         chosen = ancestors[cycle]
         mine = lax.dynamic_slice_in_dim(chosen, member * part_dev, part_dev)
         piece = (
-            lax.all_gather(bio, "particle", axis=0, tiled=True),
+            doubled_up(bio, "particle", 0),
             lax.all_gather(wat, "particle", axis=0, tiled=True),
         )
         count = piece[0].shape[0]

time: 193 us -> 170 us (0.88)
  blocking collectives: 85.8 us -> 54.7 us
  waiting for transfers between devices: 33.8 us -> 40.6 us
  other arithmetic: 18.2 us -> 20.2 us
    all_gather x2 -> x0, blocking collectives: 29.9 us -> none  [body(): lax.all_gather(bio, 'particle', axis=0, tiled=True)]
    ppermute x0 -> x4, waiting for transfers between devices: none -> 7.32 us  [doubled_up(): theirs = lax.ppermute(grown, axis, [(d, d ^ reach) for d in range(ways)])]
    ppermute x0 -> x4, starting transfers between devices: none -> 4.22 us  [doubled_up(): theirs = lax.ppermute(grown, axis, [(d, d ^ reach) for d in range(ways)])]
    select_n x0 -> x4, other arithmetic: none -> 3.75 us  [doubled_up(): grown = jnp.where(here & reach == 0, mine_first, theirs_first)]
    psum x1, waiting for transfers between devices: 31 us -> 27.4 us  [body(): collected.append(lax.psum(partial_sums, 'particle'))]
    ppermute x4, starting transfers between devices: 11.6 us -> 8.14 us  [padded(): lax.ppermute(tail, axis, [(i, (i + 1) % count) for i in range(ends)])]
    ppermute x4, waiting for transfers between devices: 2.73 us -> 5.84 us  [padded(): lax.ppermute(head, axis, [((i + 1) % count, i) for i in range(ends)])]
    unnamed x21 -> x13, local copies, waits for them, and re-layouts: 4.85 us -> 3.26 us
  transfers between devices with their start and end apart: 9 -> 13, of which waited for: 3 -> 5; matrix products, arithmetic and copies ran while one was open for 10% -> 11% of each run, Pallas kernels for 0% -> 0%
where the time goes in v1:
time: 170 us; the launch traced here: 169 us
  blocking collectives  54.7 us (32%)
  waiting for transfers between devices  40.6 us (24%)
  other arithmetic  20.2 us (12%)
  starting transfers between devices  17.6 us (10%)
  between operations  14.9 us (9%)
  matrix products  11 us (6%)
  local copies, waits for them, and re-layouts  9.95 us (6%)
    all_gather x2, blocking collectives, body(): lax.all_gather(wat, 'particle', axis=0, tiled=True)  30.6 us
    psum x1, waiting for transfers between devices, body(): collected.append(lax.psum(partial_sums, 'particle'))  27.4 us
    psum x1, blocking collectives, body(): summed = lax.psum(misfit_local, 'tile')  14.2 us
    dot_general x4, matrix products, body(): jnp.einsum('pnkc,nkdc->pnd', nearby, flow_blocks, preferred_element_type=...  11 us
    unnamed x1, blocking collectives  9.96 us
    ppermute x4, starting transfers between devices, padded(): lax.ppermute(tail, axis, [(i, (i + 1) % count) for i in range(ends)])  8.14 us
    ppermute x4, waiting for transfers between devices, doubled_up(): theirs = lax.ppermute(grown, axis, [(d, d ^ reach) for d in range(ways)])  7.32 us
    ppermute x4, waiting for transfers between devices, padded(): lax.ppermute(head, axis, [((i + 1) % count, i) for i in range(ends)])  5.84 us
  transfers between devices with their start and end apart: 13, of which 5 were waited for; matrix products, arithmetic and copies ran while one was open for 11% of the time, Pallas kernels for 0%

profile of v1, /device:TPU:0, one launch (start us, length us, event | category | flops | bytes accessed | tf_op | source)
XLA Modules:
  0.0 169.0 jit_solution(7645181512215862912)
XLA Ops:
  7.2 3.1 %collective-permute-start = (f32[4,4096]{1,0:T(4,128)}, f32[4,4096]{1,0:T(4,128)S(1)}, u32[]{:S(2)}, u32[]{:S(2)}) collective-permute-start(f32[4,4096]{1,0:T(4,128)} %param.9), channel_id=1, source_target_pairs={{0,8},{8,0},{16,24},{24,16},{1,9},{9,1},{17,25},{25,17},{2,10},{10... | collective-permute-start | bytes 196616 | tf_op jit(solution)/shard_map/ppermute | solution.py:16
  12.1 1.5 fusion.24
  13.6 14.3 %all-gather = f32[4,4,4096]{2,1,0:T(4,128)S(1)} all-gather(f32[1,4,4096]{2,1,0:T(4,128)} %bitcast.148), channel_id=1, replica_groups=mesh['particle'=4,'tile'=8] {'particle'}, dimensions={0}, use_global_device_ids=true | all-gather | bytes 327680 | tf_op jit(solution)/shard_map/all_gather | solution.py:75
  30.6 6.5 %collective-permute-done.1 = f32[8,4096]{1,0:T(8,128)S(1)} collective-permute-done((f32[8,4096]{1,0:T(8,128)S(1)}, f32[8,4096]{1,0:T(8,128)S(1)}, u32[]{:S(2)}, u32[]{:S(2)}) %collective-permute-start.1) | collective-permute-done | bytes 131104 | tf_op jit(solution)/shard_map/ppermute | solution.py:16
  37.1 1.4 select_reduce_fusion.3
  39.9 1.3 collective-permute-start.3
  43.1 1.6 collective-permute-done.3
  44.7 1.3 gather_fusion
  46.0 3.0 %multiply_reduce_fusion.5 = (f32[4]{0:T(128)S(1)}, f32[4]{0:T(128)S(1)}, f32[4,4096]{1,0:T(4,128)S(1)}, f32[4,4096]{1,0:T(4,128)S(1)}, f32[32,4,128,1]{2,1,3,0:T(4,128)}) fusion(f32[4,4096]{1,0:T(4,128)} %param.9, f32[4096]{0:T(1024)} %bitcast.150, f32[4096]{0:T(1024)} %param.16, f32[4096]{0:T(1024)} %bitcast.149, f32[4,4096]{1,0:T(4,128)S(1)} %get-tuple-element.11, ...), kind=kOutput, calls=%fused_computation.54 | convolution fusion | flops 13058040 | bytes 3768352 | tf_op jit(solution)/shard_map/pnkc,nkdc->pnd/dot_general | solution.py:86
  49.0 14.2 %all-reduce.2 = (f32[4]{0:T(128)S(1)}, f32[4]{0:T(128)S(1)}) all-reduce(f32[4]{0:T(128)S(1)} %get-tuple-element.38, f32[4]{0:T(128)S(1)} %get-tuple-element.39), channel_id=1, replica_groups=mesh['particle'=4,'tile'=8] {'tile'}, use_global_device_ids=true, to_apply=%region_10.11 | all-reduce | flops 8 | bytes 64 | tf_op jit(solution)/shard_map/psum | solution.py:62
  63.6 10.0 %all-reduce.4 = (f32[16]{0:T(128)S(1)}, f32[16]{0:T(128)S(1)}) all-reduce(f32[16]{0:T(128)S(1)} %dynamic-update-slice.1, f32[16]{0:T(128)S(1)} %dynamic-update-slice), channel_id=1, replica_groups=mesh['particle'=4,'tile'=8] {'particle'}, use_global_device_ids=true, to_apply=%add.1 | all-reduce | flops 32 | bytes 256
  75.4 1.3 broadcast_divide_fusion.1
  81.9 1.3 collective-permute-start.5
  87.7 1.6 maximum_select_fusion.3
  89.3 2.7 %multiply_reduce_fusion.1 = (f32[4096]{0:T(1024)}, f32[4096]{0:T(1024)}, f32[4,4096]{1,0:T(4,128)S(1)}) fusion(f32[4,4096]{1,0:T(4,128)S(1)} %get-tuple-element.21, f32[4]{0:T(128)} %dynamic_slice.14, f32[4,4096]{1,0:T(4,128)S(1)} %get-tuple-element.22, f32[4,4096]{1,0:T(4,128)S(1)} %get-tuple-element.11, f32[4,4096]{1,0:T(4,128)S(1)} %get-tuple-element.12, ...), kind=kOutput, calls=%fused_computation.48 | convolution fusion | flops 12902400 | bytes 3686416 | tf_op jit(solution)/shard_map/pnkc,nkdc->pnd/dot_general | solution.py:86
  92.0 16.2 %all-gather.1 = f32[4,4,4096]{2,1,0:T(4,128)S(1)} all-gather(f32[1,4,4096]{2,1,0:T(4,128)S(1)} %bitcast.147), channel_id=1, replica_groups=mesh['particle'=4,'tile'=8] {'particle'}, dimensions={0}, use_global_device_ids=true | all-gather | bytes 327680 | tf_op jit(solution)/shard_map/all_gather | solution.py:75
  110.2 1.4 select_reduce_fusion.1
  114.2 1.4 maximum_bitcast_fusion.1
  115.7 4.3 %collective-permute-done.9 = bf16[4,4,128]{2,0,1:T(4,128)(2,1)S(1)} collective-permute-done((bf16[4,4,128]{2,0,1:T(4,128)(2,1)S(1)}, bf16[4,4,128]{2,0,1:T(4,128)(2,1)S(1)}, u32[]{:S(2)}, u32[]{:S(2)}) %collective-permute-start.9) | collective-permute-done | bytes 4128 | tf_op jit(solution)/shard_map/ppermute | solution.py:34
  120.7 2.7 %multiply_add_fusion = (f32[4,4096]{1,0:T(4,128)}, f32[4,4096]{1,0:T(4,128)S(1)}, f32[32,4,128,1]{2,1,3,0:T(4,128)S(1)}) fusion(f32[4096]{0:T(1024)} %param.14, f32[4,4096]{1,0:T(4,128)S(1)} %get-tuple-element.5, f32[4,4096]{1,0:T(4,128)S(1)} %get-tuple-element.6, f32[4,4,4096]{2,1,0:T(4,128)} %param.13, bf16[4,32,3,128]{3,0,2,1:T(4,128)(2,1)S(1)} %bitcast.146, ...), kind=kOutput, calls=%fused_computation.45 | convolution fusion | flops 12926976 | bytes 3653632 | tf_op jit(solution)/shard_map/pnkc,nkdc->pnd/dot_general | solution.py:86
  124.3 4.3 %collective-permute-start.10 = (bf16[4,4,128]{2,0,1:T(4,128)(2,1)S(1)}, bf16[4,4,128]{2,0,1:T(4,128)(2,1)S(1)}, u32[]{:S(2)}, u32[]{:S(2)}) collective-permute-start(bf16[4,4,128]{2,0,1:T(4,128)(2,1)S(1)} %get-tuple-element.23), channel_id=1, source_target_pairs={{0,1},{1,2},{2,3},{3,4},{4,5},{5,6},{6,7},{8,9},{9,10},{10,11},{11... | collective-permute-start | bytes 12296 | tf_op jit(solution)/shard_map/ppermute | solution.py:32
  129.9 27.4 %all-reduce.7.cloned.1.call-done = (f32[1,2,4096]{2,1,0:T(2,128)}, f32[1,2,4096]{2,1,0:T(2,128)}) async-done(((f32[1,2,4096]{2,1,0:T(2,128)}, f32[1,2,4096]{2,1,0:T(2,128)}), (f32[1,2,4096]{2,1,0:T(2,128)}, f32[1,2,4096]{2,1,0:T(2,128)})) %all-reduce.7.cloned.1.call-update) | async-done | bytes 65552 | tf_op jit(solution)/shard_map/psum | solution.py:70
  157.2 1.4 pad_maximum_fusion
  159.4 2.7 %fusion.2 = f32[4,4096]{1,0:T(4,128)} fusion(f32[4,4096]{1,0:T(4,128)S(1)} %get-tuple-element.20, bf16[4,32,3,128]{3,0,2,1:T(4,128)(2,1)S(1)} %bitcast.143, bf16[32,3,128,128]{3,2,1,0:T(8,128)(2,1)S(1)} %copy-done, f32[4,4,4096]{2,1,0:T(4,128)} %param.13, f32[4,4096]{1,0:T(4,128)S(1)} %get-tuple-element.5, f32[4,4096]{1,0:T(4,128)S(1)} %get-tuple-element.6, ...), kind=kOutput, calls=%fused_computation.7 | convolution fusion | flops 12845056 | bytes 3588096 | tf_op jit(solution)/shard_map/pnkc,nkdc->pnd/dot_general | solution.py:86
  (69 shorter events, 27.2 us)
Async XLA Ops:
  7.2 38.9 %copy-start = (bf16[32,3,128,128]{3,2,1,0:T(8,128)(2,1)S(1)}, bf16[32,3,128,128]{3,2,1,0:T(8,128)(2,1)}, u32[]{:S(2)}) copy-start(bf16[32,3,128,128]{3,2,1,0:T(8,128)(2,1)} %param.11) | copy-start | bytes 9437188
  7.2 150.1 %all-reduce.7.cloned.1.call-start = ((), (), s32[]{:S(2)}) async-start(), calls=%async_computation | async-start | bytes 131072 | tf_op jit(solution)/shard_map/psum | solution.py:70
  7.2 21.6 %collective-permute-start = (f32[4,4096]{1,0:T(4,128)}, f32[4,4096]{1,0:T(4,128)S(1)}, u32[]{:S(2)}, u32[]{:S(2)}) collective-permute-start(f32[4,4096]{1,0:T(4,128)} %param.9), channel_id=1, source_target_pairs={{0,8},{8,0},{16,24},{24,16},{1,9},{9,1},{17,25},{25,17},{2,10},{10... | collective-permute-start | bytes 196616 | tf_op jit(solution)/shard_map/ppermute | solution.py:16
  27.9 50.8 %copy-start.1 = (f32[4,4096]{1,0:T(4,128)S(1)}, f32[4,4096]{1,0:T(4,128)}, u32[]{:S(2)}) copy-start(f32[4,4096]{1,0:T(4,128)} %param.9) | copy-start | bytes 196612
  29.8 7.3 %collective-permute-start.1 = (f32[8,4096]{1,0:T(8,128)S(1)}, f32[8,4096]{1,0:T(8,128)S(1)}, u32[]{:S(2)}, u32[]{:S(2)}) collective-permute-start(f32[8,4096]{1,0:T(8,128)S(1)} %maximum_select_fusion.2), channel_id=1, source_target_pairs={{0,16},{8,24},{16,0},{24,8},{1,17},{9,25},{17,1},{25,9},{2,18},{10... | collective-permute-start | bytes 393224 | tf_op jit(solution)/shard_map/ppermute | solution.py:16
  38.6 4.5 %collective-permute-start.2 = (bf16[4,4,128]{2,0,1:T(4,128)(2,1)S(1)}, bf16[4,4,128]{2,0,1:T(4,128)(2,1)S(1)}, u32[]{:S(2)}, u32[]{:S(2)}) collective-permute-start(bf16[4,4,128]{2,0,1:T(4,128)(2,1)S(1)} %get-tuple-element.29), channel_id=1, source_target_pairs={{0,1},{1,2},{2,3},{3,4},{4,5},{5,6},{6,7},{8,9},{9,10},{10,11},{11... | collective-permute-start | bytes 12296 | tf_op jit(solution)/shard_map/ppermute | solution.py:32
  39.9 4.8 %collective-permute-start.3 = (bf16[4,4,128]{2,0,1:T(4,128)(2,1)S(1)}, bf16[4,4,128]{2,0,1:T(4,128)(2,1)S(1)}, u32[]{:S(2)}, u32[]{:S(2)}) collective-permute-start(bf16[4,4,128]{2,0,1:T(4,128)(2,1)S(1)} %get-tuple-element.30), channel_id=1, source_target_pairs={{1,0},{2,1},{3,2},{4,3},{5,4},{6,5},{7,6},{9,8},{10,9},{11,10},{12... | collective-permute-start | bytes 12296 | tf_op jit(solution)/shard_map/ppermute | solution.py:34
  80.6 5.5 %collective-permute-start.4 = (bf16[4,4,128]{2,0,1:T(4,128)(2,1)S(1)}, bf16[4,4,128]{2,0,1:T(4,128)(2,1)S(1)}, u32[]{:S(2)}, u32[]{:S(2)}) collective-permute-start(bf16[4,4,128]{2,0,1:T(4,128)(2,1)S(1)} %get-tuple-element.27), channel_id=1, source_target_pairs={{0,1},{1,2},{2,3},{3,4},{4,5},{5,6},{6,7},{8,9},{9,10},{10,11},{11... | collective-permute-start | bytes 12296 | tf_op jit(solution)/shard_map/ppermute | solution.py:32
  81.9 4.2 %collective-permute-start.5 = (bf16[4,4,128]{2,0,1:T(4,128)(2,1)S(1)}, bf16[4,4,128]{2,0,1:T(4,128)(2,1)S(1)}, u32[]{:S(2)}, u32[]{:S(2)}) collective-permute-start(bf16[4,4,128]{2,0,1:T(4,128)(2,1)S(1)} %get-tuple-element.28), channel_id=1, source_target_pairs={{1,0},{2,1},{3,2},{4,3},{5,4},{6,5},{7,6},{9,8},{10,9},{11,10},{12... | collective-permute-start | bytes 12296 | tf_op jit(solution)/shard_map/ppermute | solution.py:34
  83.2 4.4 %collective-permute-start.6 = (f32[4,4096]{1,0:T(4,128)S(1)}, f32[4,4096]{1,0:T(4,128)}, u32[]{:S(2)}, u32[]{:S(2)}) collective-permute-start(f32[4,4096]{1,0:T(4,128)S(1)} %get-tuple-element.21), channel_id=1, source_target_pairs={{0,8},{8,0},{16,24},{24,16},{1,9},{9,1},{17,25},{25,17},{2,10},{10... | collective-permute-start | bytes 196616 | tf_op jit(solution)/shard_map/ppermute | solution.py:16
  89.3 19.7 %collective-permute-start.7 = (f32[8,4096]{1,0:T(8,128)}, f32[8,4096]{1,0:T(8,128)}, u32[]{:S(2)}, u32[]{:S(2)}) collective-permute-start(f32[8,4096]{1,0:T(8,128)} %maximum_select_fusion.3), channel_id=1, source_target_pairs={{0,16},{8,24},{16,0},{24,8},{1,17},{9,25},{17,1},{25,9},{2,18},{10... | collective-permute-start | bytes 393224 | tf_op jit(solution)/shard_map/ppermute | solution.py:16
  109.0 50.4 %copy-start.2 = (f32[4096]{0:T(1024)S(1)}, f32[4096]{0:T(1024)}, u32[]{:S(2)}) copy-start(f32[4096]{0:T(1024)} %param.14) | copy-start | bytes 49156
  111.6 4.0 %collective-permute-start.8 = (bf16[4,4,128]{2,0,1:T(4,128)(2,1)S(1)}, bf16[4,4,128]{2,0,1:T(4,128)(2,1)S(1)}, u32[]{:S(2)}, u32[]{:S(2)}) collective-permute-start(bf16[4,4,128]{2,0,1:T(4,128)(2,1)S(1)} %get-tuple-element.25), channel_id=1, source_target_pairs={{0,1},{1,2},{2,3},{3,4},{4,5},{5,6},{6,7},{8,9},{9,10},{10,11},{11... | collective-permute-start | bytes 12296 | tf_op jit(solution)/shard_map/ppermute | solution.py:32
  112.9 7.0 %collective-permute-start.9 = (bf16[4,4,128]{2,0,1:T(4,128)(2,1)S(1)}, bf16[4,4,128]{2,0,1:T(4,128)(2,1)S(1)}, u32[]{:S(2)}, u32[]{:S(2)}) collective-permute-start(bf16[4,4,128]{2,0,1:T(4,128)(2,1)S(1)} %get-tuple-element.26), channel_id=1, source_target_pairs={{1,0},{2,1},{3,2},{4,3},{5,4},{6,5},{7,6},{9,8},{10,9},{11,10},{12... | collective-permute-start | bytes 12296 | tf_op jit(solution)/shard_map/ppermute | solution.py:34
  124.3 34.4 %collective-permute-start.10 = (bf16[4,4,128]{2,0,1:T(4,128)(2,1)S(1)}, bf16[4,4,128]{2,0,1:T(4,128)(2,1)S(1)}, u32[]{:S(2)}, u32[]{:S(2)}) collective-permute-start(bf16[4,4,128]{2,0,1:T(4,128)(2,1)S(1)} %get-tuple-element.23), channel_id=1, source_target_pairs={{0,1},{1,2},{2,3},{3,4},{4,5},{5,6},{6,7},{8,9},{9,10},{10,11},{11... | collective-permute-start | bytes 12296 | tf_op jit(solution)/shard_map/ppermute | solution.py:32
  128.6 30.1 %collective-permute-start.11 = (bf16[4,4,128]{2,0,1:T(4,128)(2,1)S(1)}, bf16[4,4,128]{2,0,1:T(4,128)(2,1)S(1)}, u32[]{:S(2)}, u32[]{:S(2)}) collective-permute-start(bf16[4,4,128]{2,0,1:T(4,128)(2,1)S(1)} %get-tuple-element.24), channel_id=1, source_target_pairs={{1,0},{2,1},{3,2},{4,3},{5,4},{6,5},{7,6},{9,8},{10,9},{11,10},{12... | collective-permute-start | bytes 12296 | tf_op jit(solution)/shard_map/ppermute | solution.py:34
Sparse Core Ops, SparseCore 0:
  115.8 41.4 all-reduce.6
